TPU v7x, 32 devices: a whole 2x2x4 slice. The times are simulated.
32 devices in a mesh: blk: 8 (over z, x), rep: 4 (over y, core).
Axes of the slice: x: 2, y: 2, z: 4, core: 2. Of those that a mesh axis runs over, the one named last changes fastest.
Arguments:
- node_feats: bfloat16 [16384, 128], P(('blk', 'rep')), may hold values from -6 to 6
- adj_tiles: bfloat16 [128, 4, 4, 128, 128], P('blk', 'rep'), as said below
- col_index: int32 [128, 4, 4], P('blk', 'rep'), may hold values from 0 to 31, as said below
- w_in: bfloat16 [128, 512], replicated, may hold values from -0.5 to 0.5
- b_in: float32 [512], replicated, may hold values from -3 to 3
- w_out: bfloat16 [512, 128], replicated, may hold values from -0.25 to 0.25
- b_out: float32 [128], replicated, may hold values from -3 to 3
- cot_out: bfloat16 [16384, 128], P(('blk', 'rep')), may hold values from -6 to 6
Outputs:
- out_feats: bfloat16 [16384, 128], P(('blk', 'rep'))
- grad_feats: bfloat16 [16384, 128], P(('blk', 'rep'))
Inputs may be any that keep to these rules, and one draw needn't show every extreme that they name: The matrix A described by adj_tiles and col_index is symmetric (A equals its transpose). `col_index`: column block numbers within a quarter.
All inputs are finite; a program needn't handle non-finite values.
Results may differ from a plain program's by a relative error of at most 0.0045.
Values may be sent and summed in bfloat16 or wider, within the bound.
No kernel may reach another device: no remote copies, remote signals or barrier semaphores. Data moves between devices by JAX's collectives and lax.ppermute only.
A program may use at most 128 MiB of HBM per device.

v0:
```python
import functools

import jax
import jax.numpy as jnp
from jax import lax
from jax.experimental import pallas as pl
from jax.experimental.pallas import tpu as pltpu
from jax.sharding import PartitionSpec as P

BLOCK = 128
VMEM = pl.BlockSpec(memory_space=pltpu.VMEM)


BESIDE = 2 * 10**10
PAIRS = 4


def after(pair):
    return (3 * pair + 2) % (PAIRS + 1)


def before(pair):
    return (2 * pair + 1) % (PAIRS + 1)


def gather_blocks(rows):
    n = lax.axis_size("blk")
    if n != 2 * PAIRS:
        return [("all", lax.all_gather(rows, "blk", axis=0, tiled=True))]

    def beside(piece):
        return lax.ppermute(piece, "blk", [(i, i ^ 1) for i in range(n)])

    def step(piece, hop):
        return lax.ppermute(piece, "blk", [(i, 2 * hop(i // 2) + i % 2) for i in range(n)])

    first, second, own_beside = step(rows, after), step(rows, before), beside(rows)
    first_beside = beside(first)
    third = step(lax.optimization_barrier((first, own_beside))[0], after)
    third_beside = step(first_beside, after)
    second_beside = beside(second)
    return [
        ("own", rows),
        ("own beside", own_beside),
        ("second", second),
        ("second beside", second_beside),
        ("third", third),
        ("third beside", third_beside),
        ("first", first),
        ("first beside", first_beside),
    ]


def place_pieces(panel, blk, rows, names, pieces):
    got = dict(zip(names, pieces))
    if "all" in got:
        panel[...] = got["all"][...]
        return
    pair, side = blk // 2, lax.rem(blk, 2)
    came = {"own": pair, "first": before(pair), "second": after(pair), "third": before(before(pair))}
    for name, source in came.items():
        for which, other in ((name, 0), (name + " beside", 1)):
            start = (2 * source + lax.bitwise_xor(side, other)) * rows
            panel[pl.ds(pl.multiple_of(start, rows), rows), :] = got[which][...]


def add_blocks(columns, tiles, panel, out, owners):
    per_owner = out.shape[0] // (BLOCK * len(owners))
    slots_here = range(tiles.shape[2])
    for j, owner in enumerate(owners):
        numbers = columns[pl.ds(owner * per_owner, per_owner), :]
        for i in range(per_owner):
            starts = [pl.multiple_of(numbers[i, k] * BLOCK, BLOCK) for k in slots_here]
            left = jnp.concatenate([tiles[owner * per_owner + i, 0, k] for k in slots_here], axis=1)
            right = jnp.concatenate([panel[pl.ds(start, BLOCK), :] for start in starts], axis=0)
            summed = jnp.dot(left, right, preferred_element_type=jnp.float32)
            out[pl.ds((j * per_owner + i) * BLOCK, BLOCK), :] = summed.astype(out.dtype)


def other_kernel(names, reps, columns, tiles, *refs):
    pieces, panel, out = refs[: len(names)], refs[-2], refs[-1]
    blk, rep = lax.axis_index("blk"), lax.axis_index("rep")
    place_pieces(panel, blk, tiles.shape[0] * BLOCK // reps, names, pieces)
    add_blocks(columns, tiles, panel, out, [lax.bitwise_xor(rep, d) for d in range(3, reps, 2)])


def other_sums(gathered, adj_tiles, columns):
    reps = lax.axis_size("rep")
    names, pieces = zip(*gathered)
    width = pieces[0].shape[1]
    rows = adj_tiles.shape[0] * BLOCK // reps
    length = lax.axis_size("blk") * rows
    return pl.pallas_call(
        functools.partial(other_kernel, names, reps),
        out_shape=[
            jax.ShapeDtypeStruct((length, width), jnp.bfloat16),
            jax.ShapeDtypeStruct((rows * (reps // 2 - 1), width), jnp.bfloat16),
        ],
        in_specs=[VMEM, VMEM] + [VMEM] * len(pieces),
        out_specs=[VMEM] * 2,
        compiler_params=pltpu.CompilerParams(vmem_limit_bytes=32 * 1024 * 1024),
        cost_estimate=product_cost(adj_tiles, width, reps),
        name="other_sums",
    )(columns, adj_tiles, *pieces)


def sums_kernel(owners, columns, tiles, panel, out):
    rep = lax.axis_index("rep")
    add_blocks(columns, tiles, panel, out, [lax.bitwise_xor(rep, d) for d in owners])


def sums(panel, adj_tiles, columns, owners, kind, name):
    reps = lax.axis_size("rep")
    rows, width = adj_tiles.shape[0] * BLOCK // reps * len(owners), panel.shape[1]
    return pl.pallas_call(
        functools.partial(sums_kernel, owners),
        out_shape=jax.ShapeDtypeStruct((rows, width), kind),
        in_specs=[VMEM, VMEM, VMEM],
        out_specs=VMEM,
        compiler_params=pltpu.CompilerParams(vmem_limit_bytes=32 * 1024 * 1024),
        cost_estimate=product_cost(adj_tiles, width, reps),
        name=name,
    )(columns, adj_tiles, panel)


def product_cost(adj_tiles, width, reps):
    size = adj_tiles.size // reps
    return pl.CostEstimate(flops=2 * size * width, bytes_accessed=2 * size, transcendentals=0)


def add_cores_kernel(own, core, *outs):
    rows = outs[0].shape[0]
    for j, out in enumerate(outs):
        part = pl.ds(j * rows, rows)
        out[...] = (own[part, :] + core[part, :].astype(jnp.float32)).astype(jnp.bfloat16)


def add_cores(own, core, rows):
    width = own.shape[1]
    return pl.pallas_call(
        add_cores_kernel,
        out_shape=[jax.ShapeDtypeStruct((rows, width), jnp.bfloat16)] * (own.shape[0] // rows),
        in_specs=[VMEM] * 2,
        out_specs=[VMEM] * (own.shape[0] // rows),
        compiler_params=pltpu.CompilerParams(vmem_limit_bytes=32 * 1024 * 1024),
        name="add_cores",
    )(own, core)


def tile_products(pieces, adj_tiles, columns, rows):
    reps = lax.axis_size("rep")
    other = [(i, i ^ 1) for i in range(reps)]
    panel, across = other_sums(pieces, adj_tiles, columns)
    core = lax.ppermute(across, "rep", other)
    own = sums(panel, adj_tiles, columns, range(2, reps, 2), jnp.float32, "own_far")
    parts = add_cores(own, core, rows)
    panel, parts = lax.optimization_barrier((panel, parts))
    far = []
    for j, part in enumerate(parts, 1):
        far.append(lax.ppermute(part, "rep", [(i, i ^ (2 * j)) for i in range(reps)]))
    near = sums(panel, adj_tiles, columns, [0], jnp.float32, "own_near")
    panel, near = lax.optimization_barrier((panel, near))
    beside = lax.ppermute(sums(panel, adj_tiles, columns, [1], jnp.bfloat16, "near_other"), "rep", other)
    terms = [near, *far, beside]
    return terms


def add_terms(terms, rows):
    total = terms[0][...].astype(jnp.float32)
    for term in terms[1:]:
        total = total + term[...].astype(jnp.float32)
    return total


def contract(a, b, dims):
    return lax.dot_general(a, b, ((dims[:1], dims[1:]), ((), ())), preferred_element_type=jnp.float32)


def by_row_kernel(by_slot, columns):
    columns[...] = jnp.zeros_like(columns)
    columns[pl.ds(0, by_slot.shape[1]), :] = jnp.transpose(by_slot[...])


def by_row(by_slot):
    per_row, rows = by_slot.shape
    return pl.pallas_call(
        by_row_kernel,
        out_shape=jax.ShapeDtypeStruct((rows + 8, per_row), jnp.int32),
        in_specs=[VMEM],
        out_specs=VMEM,
        compiler_params=pltpu.CompilerParams(vmem_limit_bytes=32 * 1024 * 1024),
        cost_estimate=pl.CostEstimate(flops=BESIDE, bytes_accessed=by_slot.size, transcendentals=0),
        name="by_row",
    )(by_slot)


def early_kernel(cot, w_out, g_hidden):
    g_hidden[...] = contract(cot[...], w_out[...], (1, 1))


def early(cot_out, w_out):
    rows, width = cot_out.shape
    units = w_out.shape[0]
    return pl.pallas_call(
        early_kernel,
        out_shape=jax.ShapeDtypeStruct((rows, units), jnp.float32),
        in_specs=[VMEM] * 2,
        out_specs=VMEM,
        compiler_params=pltpu.CompilerParams(vmem_limit_bytes=32 * 1024 * 1024),
        cost_estimate=pl.CostEstimate(
            flops=2 * rows * width * units, bytes_accessed=8 * rows * units, transcendentals=0
        ),
        name="early",
    )(cot_out, w_out)


def node_pre(terms, rows, w_in, b_in):
    agg_b = add_terms(terms, rows).astype(jnp.bfloat16)
    pre = contract(agg_b, w_in[...], (1, 0)) + b_in[...]
    return pre, 1.0 / (1.0 + jnp.exp(-pre))


def node_kernel(n_terms, *refs):
    terms = refs[:n_terms]
    g_hidden, w_in, b_in, g_out = refs[n_terms:]
    pre, sigma = node_pre(terms, g_out.shape[0], w_in, b_in)
    g_pre = (g_hidden[...] * sigma * (1.0 + pre * (1.0 - sigma))).astype(jnp.bfloat16)
    g_out[...] = contract(g_pre, w_in[...], (1, 1)).astype(jnp.bfloat16)


def node_update(terms, g_hidden, w_in, b_in):
    rows, units = g_hidden.shape
    width = w_in.shape[0]
    return pl.pallas_call(
        functools.partial(node_kernel, len(terms)),
        out_shape=jax.ShapeDtypeStruct((rows, width), jnp.bfloat16),
        in_specs=[VMEM] * (len(terms) + 3),
        out_specs=VMEM,
        compiler_params=pltpu.CompilerParams(vmem_limit_bytes=32 * 1024 * 1024),
        cost_estimate=pl.CostEstimate(
            flops=4 * rows * width * units, bytes_accessed=8 * rows * units, transcendentals=rows * units
        ),
        name="node_update",
    )(*terms, g_hidden, w_in, b_in.reshape(1, -1))


def project_kernel(n_terms, *refs):
    terms = refs[:n_terms]
    feats, w_in, b_in, w_out, b_out, out = refs[n_terms:]
    pre, sigma = node_pre(terms, out.shape[0], w_in, b_in)
    projected = contract((pre * sigma).astype(jnp.bfloat16), w_out[...], (1, 0)) + b_out[...]
    out[...] = (feats[...].astype(jnp.float32) + projected).astype(jnp.bfloat16)


def project(terms, node_feats, w_in, b_in, w_out, b_out):
    rows, width = node_feats.shape
    units = w_in.shape[1]
    return pl.pallas_call(
        functools.partial(project_kernel, len(terms)),
        out_shape=jax.ShapeDtypeStruct((rows, width), jnp.bfloat16),
        in_specs=[VMEM] * (len(terms) + 5),
        out_specs=VMEM,
        compiler_params=pltpu.CompilerParams(vmem_limit_bytes=32 * 1024 * 1024),
        cost_estimate=pl.CostEstimate(
            flops=4 * rows * width * units, bytes_accessed=2 * rows * units, transcendentals=rows * units
        ),
        name="project",
    )(*terms, node_feats, w_in, b_in.reshape(1, -1), w_out, b_out.reshape(1, -1))


def close_kernel(n_terms, *refs):
    cot, out = refs[n_terms:]
    total = add_terms(refs[:n_terms], out.shape[0])
    out[...] = (cot[...].astype(jnp.float32) + total).astype(jnp.bfloat16)


def close_grad(terms, cot_out):
    return pl.pallas_call(
        functools.partial(close_kernel, len(terms)),
        out_shape=jax.ShapeDtypeStruct(cot_out.shape, jnp.bfloat16),
        in_specs=[VMEM] * (len(terms) + 1),
        out_specs=VMEM,
        compiler_params=pltpu.CompilerParams(vmem_limit_bytes=32 * 1024 * 1024),
        name="close_grad",
    )(*terms, cot_out)


def local(node_feats, adj_tiles, col_index, w_in, b_in, w_out, b_out, cot_out):
    rows = node_feats.shape[0]
    columns = by_row(jnp.transpose(col_index, (1, 2, 0))[0])
    g_hidden = early(cot_out, lax.optimization_barrier((w_out, columns))[0])
    columns, g_hidden = lax.optimization_barrier((columns, g_hidden))
    terms = tile_products(gather_blocks(node_feats), adj_tiles, columns, rows)
    g_agg = node_update(terms, g_hidden, w_in, b_in)
    out_feats = project(terms, node_feats, w_in, b_in, w_out, b_out)
    terms = tile_products(gather_blocks(g_agg), adj_tiles, columns, rows)
    return (out_feats, close_grad(terms, cot_out))


def solution(mesh):
    placed = (
        P(("blk", "rep"), None),
        P("blk", "rep", None, None, None),
        P("blk", "rep", None),
        P(),
        P(),
        P(),
        P(),
        P(("blk", "rep"), None),
    )
    return jax.shard_map(
        local,
        mesh=mesh,
        in_specs=placed,
        out_specs=(P(("blk", "rep"), None), P(("blk", "rep"), None)),
        check_vma=False,
    )
```

profile of v0, /device:TPU:0, one launch (start us, length us, event | category | flops | bytes accessed | tf_op | source)
XLA Modules:
  0.0 54.8 jit_solution(4651427211113911834)
XLA Ops:
  0.6 4.1 %collective-permute-start.3 = (bf16[512,128]{1,0:T(8,128)(2,1)}, bf16[512,128]{1,0:T(8,128)(2,1)S(1)}, u32[]{:S(2)}, u32[]{:S(2)}) collective-permute-start(bf16[512,128]{1,0:T(8,128)(2,1)} %refs_3_.2), channel_id=1, source_target_pairs={{0,16},{4,20},{8,0},{12,4},{16,24},{20,28},{24,8},{28,12},{1,17},{... | collective-permute-start | bytes 393224 | tf_op jit(solution)/shard_map/ppermute | solution.py:35
  4.7 1.5 %collective-permute-start = (bf16[512,128]{1,0:T(8,128)(2,1)}, bf16[512,128]{1,0:T(8,128)(2,1)S(1)}, u32[]{:S(2)}, u32[]{:S(2)}) collective-permute-start(bf16[512,128]{1,0:T(8,128)(2,1)} %refs_3_.2), channel_id=1, source_target_pairs={{0,4},{4,0},{8,12},{12,8},{16,20},{20,16},{24,28},{28,24},{1,5},{5... | collective-permute-start | bytes 393224 | tf_op jit(solution)/shard_map/ppermute | solution.py:32
  6.2 0.0 collective-permute-start.1
  6.2 2.7 %collective-permute-done.3.refs_6_ = bf16[512,128]{1,0:T(8,128)(2,1)S(1)} collective-permute-done((bf16[512,128]{1,0:T(8,128)(2,1)}, bf16[512,128]{1,0:T(8,128)(2,1)S(1)}, u32[]{:S(2)}, u32[]{:S(2)}) %collective-permute-start.3) | collective-permute-done | bytes 131104 | tf_op jit(solution)/shard_map/ppermute | solution.py:35
  8.9 1.5 %collective-permute-start.5 = (bf16[512,128]{1,0:T(8,128)(2,1)S(1)}, bf16[512,128]{1,0:T(8,128)(2,1)S(1)}, u32[]{:S(2)}, u32[]{:S(2)}) collective-permute-start(bf16[512,128]{1,0:T(8,128)(2,1)S(1)} %collective-permute-done.3.refs_6_), channel_id=1, source_target_pairs={{0,4},{4,0},{8,12},{12,8},{16,20},{20,16},{24,28},{28,24},{1,5},{5... | collective-permute-start | bytes 393224 | tf_op jit(solution)/shard_map/ppermute | solution.py:32
  10.4 0.0 collective-permute-done.refs_1_
  10.5 3.2 %collective-permute-start.4 = (bf16[512,128]{1,0:T(8,128)(2,1)S(1)}, bf16[512,128]{1,0:T(8,128)(2,1)S(1)}, u32[]{:S(2)}, u32[]{:S(2)}) collective-permute-start(bf16[512,128]{1,0:T(8,128)(2,1)S(1)} %collective-permute-done.3.refs_6_), channel_id=1, source_target_pairs={{0,16},{4,20},{8,0},{12,4},{16,24},{20,28},{24,8},{28,12},{1,17},{... | collective-permute-start | bytes 393224 | tf_op jit(solution)/shard_map/ppermute | solution.py:35
  13.7 0.0 collective-permute-done.1.refs_2_
  13.7 0.5 collective-permute-start.2
  14.2 0.0 collective-permute-done.5.refs_7_
  14.3 2.9 %collective-permute-start.6 = (bf16[512,128]{1,0:T(8,128)(2,1)S(1)}, bf16[512,128]{1,0:T(8,128)(2,1)S(1)}, u32[]{:S(2)}, u32[]{:S(2)}) collective-permute-start(bf16[512,128]{1,0:T(8,128)(2,1)S(1)} %collective-permute-done.5.refs_7_), channel_id=1, source_target_pairs={{0,16},{4,20},{8,0},{12,4},{16,24},{20,28},{24,8},{28,12},{1,17},{... | collective-permute-start | bytes 393224 | tf_op jit(solution)/shard_map/ppermute | solution.py:35
  17.2 0.7 %copy-done.7 = s32[16,1,4]{0,2,1:T(4,128)S(1)} copy-done((s32[16,1,4]{0,2,1:T(4,128)S(1)}, s32[16,1,4]{0,2,1:T(4,128)}, u32[]{:S(2)}) %copy-start.7) | copy-done | bytes 280
  17.9 0.1 by_row.1.columns
  17.9 0.8 %copy-done.1 = bf16[512,128]{1,0:T(8,128)(2,1)S(1)} copy-done((bf16[512,128]{1,0:T(8,128)(2,1)S(1)}, bf16[512,128]{1,0:T(8,128)(2,1)}, u32[]{:S(2)}) %copy-start.1) | copy-done | bytes 131096
  18.8 0.1 copy-done.4
  18.8 0.3 early.1.refs_3_
  19.1 0.0 collective-permute-done.2.refs_3_
  19.1 0.0 collective-permute-done.4.refs_4_
  19.1 0.6 %collective-permute-done.6.refs_5_ = bf16[512,128]{1,0:T(8,128)(2,1)S(1)} collective-permute-done((bf16[512,128]{1,0:T(8,128)(2,1)S(1)}, bf16[512,128]{1,0:T(8,128)(2,1)S(1)}, u32[]{:S(2)}, u32[]{:S(2)}) %collective-permute-start.6) | collective-permute-done | bytes 131104 | tf_op jit(solution)/shard_map/ppermute | solution.py:35
  19.7 0.0 copy-done
  19.7 0.0 copy-done.2
  19.7 0.4 other_sums.2
  20.1 0.1 collective-permute-start.7
  20.2 0.4 own_far.2.own
  20.6 0.9 %collective-permute-done.7.core = bf16[512,128]{1,0:T(8,128)(2,1)S(1)} collective-permute-done((bf16[512,128]{1,0:T(8,128)(2,1)S(1)}, bf16[512,128]{1,0:T(8,128)(2,1)S(1)}, u32[]{:S(2)}, u32[]{:S(2)}) %collective-permute-start.7) | collective-permute-done | bytes 131104 | tf_op jit(solution)/shard_map/ppermute | solution.py:154
  21.6 1.6 %collective-permute-start.8 = (bf16[512,128]{1,0:T(8,128)(2,1)S(1)}, bf16[512,128]{1,0:T(8,128)(2,1)S(1)}, u32[]{:S(2)}, u32[]{:S(2)}) collective-permute-start(bf16[512,128]{1,0:T(8,128)(2,1)S(1)} %add_cores.2), channel_id=1, source_target_pairs={{0,2},{1,3},{2,0},{3,1},{4,6},{5,7},{6,4},{7,5},{8,10},{9,11},{10,... | collective-permute-start | bytes 393224 | tf_op jit(solution)/shard_map/ppermute | solution.py:160
  23.2 0.4 own_near.2.refs_0_
  23.6 0.0 copy-start.3
  23.6 0.0 copy-start.5
  23.6 0.4 near_other.2
  24.0 0.1 collective-permute-start.9
  24.1 3.1 %collective-permute-done.8.refs_1_ = bf16[512,128]{1,0:T(8,128)(2,1)S(1)} collective-permute-done((bf16[512,128]{1,0:T(8,128)(2,1)S(1)}, bf16[512,128]{1,0:T(8,128)(2,1)S(1)}, u32[]{:S(2)}, u32[]{:S(2)}) %collective-permute-start.8) | collective-permute-done | bytes 131104 | tf_op jit(solution)/shard_map/ppermute | solution.py:160
  27.2 0.0 collective-permute-done.9.refs_2_
  27.2 0.0 copy-done.3
  27.2 0.0 copy-done.5
  27.2 0.7 %node_update.1.refs_0_ = bf16[512,128]{1,0:T(8,128)(2,1)S(1)} custom-call(f32[512,128]{1,0:T(8,128)S(1)} %own_near.2.refs_0_, bf16[512,128]{1,0:T(8,128)(2,1)S(1)} %collective-permute-done.8.refs_1_, bf16[512,128]{1,0:T(8,128)(2,1)S(1)} %collective-permute-done.9.refs_2_, f32[512,512]{1,0:T(8,128)S(1)} %early.1.refs_3_, bf16[128,512]{1,0:T(8,128)(2,1)S(1)} %copy-done.3, ...), custom_call_target="tpu_custom_call" | custom-call | flops 134217728 | bytes 2097152 | tf_op jit(solution)/shard_map/node_update/pallas_call | solution.py:234
  27.9 3.4 %collective-permute-start.13 = (bf16[512,128]{1,0:T(8,128)(2,1)S(1)}, bf16[512,128]{1,0:T(8,128)(2,1)S(1)}, u32[]{:S(2)}, u32[]{:S(2)}) collective-permute-start(bf16[512,128]{1,0:T(8,128)(2,1)S(1)} %node_update.1.refs_0_), channel_id=1, source_target_pairs={{0,16},{4,20},{8,0},{12,4},{16,24},{20,28},{24,8},{28,12},{1,17},{... | collective-permute-start | bytes 393224 | tf_op jit(solution)/shard_map/ppermute | solution.py:35
  31.3 1.5 %collective-permute-start.10 = (bf16[512,128]{1,0:T(8,128)(2,1)S(1)}, bf16[512,128]{1,0:T(8,128)(2,1)S(1)}, u32[]{:S(2)}, u32[]{:S(2)}) collective-permute-start(bf16[512,128]{1,0:T(8,128)(2,1)S(1)} %node_update.1.refs_0_), channel_id=1, source_target_pairs={{0,4},{4,0},{8,12},{12,8},{16,20},{20,16},{24,28},{28,24},{1,5},{5... | collective-permute-start | bytes 393224 | tf_op jit(solution)/shard_map/ppermute | solution.py:32
  32.9 0.2 collective-permute-start.11
  33.1 2.0 %collective-permute-done.13.refs_6_ = bf16[512,128]{1,0:T(8,128)(2,1)S(1)} collective-permute-done((bf16[512,128]{1,0:T(8,128)(2,1)S(1)}, bf16[512,128]{1,0:T(8,128)(2,1)S(1)}, u32[]{:S(2)}, u32[]{:S(2)}) %collective-permute-start.13) | collective-permute-done | bytes 131104 | tf_op jit(solution)/shard_map/ppermute | solution.py:35
  35.1 1.4 %collective-permute-start.15 = (bf16[512,128]{1,0:T(8,128)(2,1)S(1)}, bf16[512,128]{1,0:T(8,128)(2,1)S(1)}, u32[]{:S(2)}, u32[]{:S(2)}) collective-permute-start(bf16[512,128]{1,0:T(8,128)(2,1)S(1)} %collective-permute-done.13.refs_6_), channel_id=1, source_target_pairs={{0,4},{4,0},{8,12},{12,8},{16,20},{20,16},{24,28},{28,24},{1,5},{5... | collective-permute-start | bytes 393224 | tf_op jit(solution)/shard_map/ppermute | solution.py:32
  36.5 0.9 %collective-permute-done.10.refs_1_ = bf16[512,128]{1,0:T(8,128)(2,1)S(1)} collective-permute-done((bf16[512,128]{1,0:T(8,128)(2,1)S(1)}, bf16[512,128]{1,0:T(8,128)(2,1)S(1)}, u32[]{:S(2)}, u32[]{:S(2)}) %collective-permute-start.10) | collective-permute-done | bytes 131104 | tf_op jit(solution)/shard_map/ppermute | solution.py:32
  37.4 2.5 %collective-permute-start.14 = (bf16[512,128]{1,0:T(8,128)(2,1)S(1)}, bf16[512,128]{1,0:T(8,128)(2,1)S(1)}, u32[]{:S(2)}, u32[]{:S(2)}) collective-permute-start(bf16[512,128]{1,0:T(8,128)(2,1)S(1)} %collective-permute-done.13.refs_6_), channel_id=1, source_target_pairs={{0,16},{4,20},{8,0},{12,4},{16,24},{20,28},{24,8},{28,12},{1,17},{... | collective-permute-start | bytes 393224 | tf_op jit(solution)/shard_map/ppermute | solution.py:35
  39.9 0.0 collective-permute-done.11.refs_2_
  39.9 1.7 %collective-permute-start.12 = (bf16[512,128]{1,0:T(8,128)(2,1)S(1)}, bf16[512,128]{1,0:T(8,128)(2,1)S(1)}, u32[]{:S(2)}, u32[]{:S(2)}) collective-permute-start(bf16[512,128]{1,0:T(8,128)(2,1)S(1)} %collective-permute-done.11.refs_2_), channel_id=1, source_target_pairs={{0,4},{4,0},{8,12},{12,8},{16,20},{20,16},{24,28},{28,24},{1,5},{5... | collective-permute-start | bytes 393224 | tf_op jit(solution)/shard_map/ppermute | solution.py:32
  41.6 0.0 collective-permute-done.15.refs_7_
  41.6 2.3 %collective-permute-start.16 = (bf16[512,128]{1,0:T(8,128)(2,1)S(1)}, bf16[512,128]{1,0:T(8,128)(2,1)S(1)}, u32[]{:S(2)}, u32[]{:S(2)}) collective-permute-start(bf16[512,128]{1,0:T(8,128)(2,1)S(1)} %collective-permute-done.15.refs_7_), channel_id=1, source_target_pairs={{0,16},{4,20},{8,0},{12,4},{16,24},{20,28},{24,8},{28,12},{1,17},{... | collective-permute-start | bytes 393224 | tf_op jit(solution)/shard_map/ppermute | solution.py:35
  43.9 1.0 %collective-permute-done.12.refs_3_ = bf16[512,128]{1,0:T(8,128)(2,1)S(1)} collective-permute-done((bf16[512,128]{1,0:T(8,128)(2,1)S(1)}, bf16[512,128]{1,0:T(8,128)(2,1)S(1)}, u32[]{:S(2)}, u32[]{:S(2)}) %collective-permute-start.12) | collective-permute-done | bytes 131104 | tf_op jit(solution)/shard_map/ppermute | solution.py:32
  44.9 0.0 collective-permute-done.14.refs_4_
  44.9 1.7 %collective-permute-done.16.refs_5_ = bf16[512,128]{1,0:T(8,128)(2,1)S(1)} collective-permute-done((bf16[512,128]{1,0:T(8,128)(2,1)S(1)}, bf16[512,128]{1,0:T(8,128)(2,1)S(1)}, u32[]{:S(2)}, u32[]{:S(2)}) %collective-permute-start.16) | collective-permute-done | bytes 131104 | tf_op jit(solution)/shard_map/ppermute | solution.py:35
  46.6 0.4 other_sums.3
  47.0 0.1 collective-permute-start.17
  47.1 0.4 own_far.3.own
  47.5 0.9 %collective-permute-done.17.core = bf16[512,128]{1,0:T(8,128)(2,1)S(1)} collective-permute-done((bf16[512,128]{1,0:T(8,128)(2,1)S(1)}, bf16[512,128]{1,0:T(8,128)(2,1)S(1)}, u32[]{:S(2)}, u32[]{:S(2)}) %collective-permute-start.17) | collective-permute-done | bytes 131104 | tf_op jit(solution)/shard_map/ppermute | solution.py:154
  48.4 1.6 %collective-permute-start.18 = (bf16[512,128]{1,0:T(8,128)(2,1)S(1)}, bf16[512,128]{1,0:T(8,128)(2,1)S(1)}, u32[]{:S(2)}, u32[]{:S(2)}) collective-permute-start(bf16[512,128]{1,0:T(8,128)(2,1)S(1)} %add_cores.3), channel_id=1, source_target_pairs={{0,2},{1,3},{2,0},{3,1},{4,6},{5,7},{6,4},{7,5},{8,10},{9,11},{10,... | collective-permute-start | bytes 393224 | tf_op jit(solution)/shard_map/ppermute | solution.py:160
  50.0 0.4 own_near.3.refs_0_
  50.4 0.0 copy-start.6
  50.4 0.4 near_other.3
  50.9 0.1 collective-permute-start.19
  50.9 0.2 copy-done.6
  51.1 1.2 %project.1 = bf16[512,128]{1,0:T(8,128)(2,1)} custom-call(f32[512,128]{1,0:T(8,128)S(1)} %own_near.2.refs_0_, bf16[512,128]{1,0:T(8,128)(2,1)S(1)} %collective-permute-done.8.refs_1_, bf16[512,128]{1,0:T(8,128)(2,1)S(1)} %collective-permute-done.9.refs_2_, bf16[512,128]{1,0:T(8,128)(2,1)S(1)} %copy-done.2, bf16[128,512]{1,0:T(8,128)(2,1)S(1)} %copy-done.3, ...), custom_call_target="tpu_custom_call" | custom-call | flops 134217728 | bytes 524288 | tf_op jit(solution)/shard_map/project/pallas_call | solution.py:258
  52.3 1.7 %collective-permute-done.18.refs_1_ = bf16[512,128]{1,0:T(8,128)(2,1)S(1)} collective-permute-done((bf16[512,128]{1,0:T(8,128)(2,1)S(1)}, bf16[512,128]{1,0:T(8,128)(2,1)S(1)}, u32[]{:S(2)}, u32[]{:S(2)}) %collective-permute-start.18) | collective-permute-done | bytes 131104 | tf_op jit(solution)/shard_map/ppermute | solution.py:160
  54.1 0.0 collective-permute-done.19.refs_2_
  54.1 0.7 %close_grad.1 = bf16[512,128]{1,0:T(8,128)(2,1)} custom-call(f32[512,128]{1,0:T(8,128)S(1)} %own_near.3.refs_0_, bf16[512,128]{1,0:T(8,128)(2,1)S(1)} %collective-permute-done.18.refs_1_, bf16[512,128]{1,0:T(8,128)(2,1)S(1)} %collective-permute-done.19.refs_2_, bf16[512,128]{1,0:T(8,128)(2,1)S(1)} %copy-done.1), custom_call_target="tpu_custom_call" | custom-call | tf_op jit(solution)/shard_map/close_grad/pallas_call | solution.py:278
  (7 shorter events, 0.1 us)
Async XLA Ops:
  0.6 8.3 %collective-permute-start.3 = (bf16[512,128]{1,0:T(8,128)(2,1)}, bf16[512,128]{1,0:T(8,128)(2,1)S(1)}, u32[]{:S(2)}, u32[]{:S(2)}) collective-permute-start(bf16[512,128]{1,0:T(8,128)(2,1)} %refs_3_.2), channel_id=1, source_target_pairs={{0,16},{4,20},{8,0},{12,4},{16,24},{20,28},{24,8},{28,12},{1,17},{... | collective-permute-start | bytes 393224 | tf_op jit(solution)/shard_map/ppermute | solution.py:35
  4.7 5.7 %collective-permute-start = (bf16[512,128]{1,0:T(8,128)(2,1)}, bf16[512,128]{1,0:T(8,128)(2,1)S(1)}, u32[]{:S(2)}, u32[]{:S(2)}) collective-permute-start(bf16[512,128]{1,0:T(8,128)(2,1)} %refs_3_.2), channel_id=1, source_target_pairs={{0,4},{4,0},{8,12},{12,8},{16,20},{20,16},{24,28},{28,24},{1,5},{5... | collective-permute-start | bytes 393224 | tf_op jit(solution)/shard_map/ppermute | solution.py:32
  6.2 7.5 %collective-permute-start.1 = (bf16[512,128]{1,0:T(8,128)(2,1)}, bf16[512,128]{1,0:T(8,128)(2,1)S(1)}, u32[]{:S(2)}, u32[]{:S(2)}) collective-permute-start(bf16[512,128]{1,0:T(8,128)(2,1)} %refs_3_.2), channel_id=1, source_target_pairs={{0,8},{4,12},{8,24},{12,28},{16,0},{20,4},{24,16},{28,20},{1,9},{5... | collective-permute-start | bytes 393224 | tf_op jit(solution)/shard_map/ppermute | solution.py:35
  8.9 5.3 %collective-permute-start.5 = (bf16[512,128]{1,0:T(8,128)(2,1)S(1)}, bf16[512,128]{1,0:T(8,128)(2,1)S(1)}, u32[]{:S(2)}, u32[]{:S(2)}) collective-permute-start(bf16[512,128]{1,0:T(8,128)(2,1)S(1)} %collective-permute-done.3.refs_6_), channel_id=1, source_target_pairs={{0,4},{4,0},{8,12},{12,8},{16,20},{20,16},{24,28},{28,24},{1,5},{5... | collective-permute-start | bytes 393224 | tf_op jit(solution)/shard_map/ppermute | solution.py:32
  10.5 8.7 %collective-permute-start.4 = (bf16[512,128]{1,0:T(8,128)(2,1)S(1)}, bf16[512,128]{1,0:T(8,128)(2,1)S(1)}, u32[]{:S(2)}, u32[]{:S(2)}) collective-permute-start(bf16[512,128]{1,0:T(8,128)(2,1)S(1)} %collective-permute-done.3.refs_6_), channel_id=1, source_target_pairs={{0,16},{4,20},{8,0},{12,4},{16,24},{20,28},{24,8},{28,12},{1,17},{... | collective-permute-start | bytes 393224 | tf_op jit(solution)/shard_map/ppermute | solution.py:35
  13.7 5.4 %collective-permute-start.2 = (bf16[512,128]{1,0:T(8,128)(2,1)S(1)}, bf16[512,128]{1,0:T(8,128)(2,1)S(1)}, u32[]{:S(2)}, u32[]{:S(2)}) collective-permute-start(bf16[512,128]{1,0:T(8,128)(2,1)S(1)} %collective-permute-done.1.refs_2_), channel_id=1, source_target_pairs={{0,4},{4,0},{8,12},{12,8},{16,20},{20,16},{24,28},{28,24},{1,5},{5... | collective-permute-start | bytes 393224 | tf_op jit(solution)/shard_map/ppermute | solution.py:32
  14.3 5.5 %collective-permute-start.6 = (bf16[512,128]{1,0:T(8,128)(2,1)S(1)}, bf16[512,128]{1,0:T(8,128)(2,1)S(1)}, u32[]{:S(2)}, u32[]{:S(2)}) collective-permute-start(bf16[512,128]{1,0:T(8,128)(2,1)S(1)} %collective-permute-done.5.refs_7_), channel_id=1, source_target_pairs={{0,16},{4,20},{8,0},{12,4},{16,24},{20,28},{24,8},{28,12},{1,17},{... | collective-permute-start | bytes 393224 | tf_op jit(solution)/shard_map/ppermute | solution.py:35
  17.2 0.7 %copy-start.7 = (s32[16,1,4]{0,2,1:T(4,128)S(1)}, s32[16,1,4]{0,2,1:T(4,128)}, u32[]{:S(2)}) copy-start(s32[16,1,4]{0,2,1:T(4,128)} %param.10) | copy-start | bytes 772
  17.9 0.9 %copy-start.1 = (bf16[512,128]{1,0:T(8,128)(2,1)S(1)}, bf16[512,128]{1,0:T(8,128)(2,1)}, u32[]{:S(2)}) copy-start(bf16[512,128]{1,0:T(8,128)(2,1)} %refs_3_.3) | copy-start | bytes 393220
  17.9 1.0 %copy-start.4 = (bf16[512,128]{1,0:T(8,128)(2,1)S(1)}, bf16[512,128]{1,0:T(8,128)(2,1)}, u32[]{:S(2)}) copy-start(bf16[512,128]{1,0:T(8,128)(2,1)} %refs_6_.1) | copy-start | bytes 393220
  17.9 1.8 %copy-start = (bf16[16,1,4,128,128]{4,3,2,1,0:T(8,128)(2,1)S(1)}, bf16[16,1,4,128,128]{4,3,2,1,0:T(8,128)(2,1)}, u32[]{:S(2)}) copy-start(bf16[16,1,4,128,128]{4,3,2,1,0:T(8,128)(2,1)} %tiles.15) | copy-start | bytes 6291460
  17.9 1.8 %copy-start.2 = (bf16[512,128]{1,0:T(8,128)(2,1)S(1)}, bf16[512,128]{1,0:T(8,128)(2,1)}, u32[]{:S(2)}) copy-start(bf16[512,128]{1,0:T(8,128)(2,1)} %refs_3_.2) | copy-start | bytes 393220
  20.1 1.4 %collective-permute-start.7 = (bf16[512,128]{1,0:T(8,128)(2,1)S(1)}, bf16[512,128]{1,0:T(8,128)(2,1)S(1)}, u32[]{:S(2)}, u32[]{:S(2)}) collective-permute-start(bf16[512,128]{1,0:T(8,128)(2,1)S(1)} %get-tuple-element.23), channel_id=1, source_target_pairs={{0,1},{1,0},{2,3},{3,2},{4,5},{5,4},{6,7},{7,6},{8,9},{9,8},{10,11... | collective-permute-start | bytes 393224 | tf_op jit(solution)/shard_map/ppermute | solution.py:154
  21.6 5.6 %collective-permute-start.8 = (bf16[512,128]{1,0:T(8,128)(2,1)S(1)}, bf16[512,128]{1,0:T(8,128)(2,1)S(1)}, u32[]{:S(2)}, u32[]{:S(2)}) collective-permute-start(bf16[512,128]{1,0:T(8,128)(2,1)S(1)} %add_cores.2), channel_id=1, source_target_pairs={{0,2},{1,3},{2,0},{3,1},{4,6},{5,7},{6,4},{7,5},{8,10},{9,11},{10,... | collective-permute-start | bytes 393224 | tf_op jit(solution)/shard_map/ppermute | solution.py:160
  23.6 3.6 %copy-start.3 = (bf16[128,512]{1,0:T(8,128)(2,1)S(1)}, bf16[128,512]{1,0:T(8,128)(2,1)}, u32[]{:S(2)}) copy-start(bf16[128,512]{1,0:T(8,128)(2,1)} %refs_4_.3) | copy-start | bytes 393220
  23.6 3.6 %copy-start.5 = (f32[512]{0:T(512)S(1)}, f32[512]{0:T(512)}, u32[]{:S(2)}) copy-start(f32[512]{0:T(512)} %param.12) | copy-start | bytes 6148
  24.0 3.2 %collective-permute-start.9 = (bf16[512,128]{1,0:T(8,128)(2,1)S(1)}, bf16[512,128]{1,0:T(8,128)(2,1)S(1)}, u32[]{:S(2)}, u32[]{:S(2)}) collective-permute-start(bf16[512,128]{1,0:T(8,128)(2,1)S(1)} %near_other.2), channel_id=1, source_target_pairs={{0,1},{1,0},{2,3},{3,2},{4,5},{5,4},{6,7},{7,6},{8,9},{9,8},{10,11... | collective-permute-start | bytes 393224 | tf_op jit(solution)/shard_map/ppermute | solution.py:163
  27.9 7.1 %collective-permute-start.13 = (bf16[512,128]{1,0:T(8,128)(2,1)S(1)}, bf16[512,128]{1,0:T(8,128)(2,1)S(1)}, u32[]{:S(2)}, u32[]{:S(2)}) collective-permute-start(bf16[512,128]{1,0:T(8,128)(2,1)S(1)} %node_update.1.refs_0_), channel_id=1, source_target_pairs={{0,16},{4,20},{8,0},{12,4},{16,24},{20,28},{24,8},{28,12},{1,17},{... | collective-permute-start | bytes 393224 | tf_op jit(solution)/shard_map/ppermute | solution.py:35
  31.3 6.1 %collective-permute-start.10 = (bf16[512,128]{1,0:T(8,128)(2,1)S(1)}, bf16[512,128]{1,0:T(8,128)(2,1)S(1)}, u32[]{:S(2)}, u32[]{:S(2)}) collective-permute-start(bf16[512,128]{1,0:T(8,128)(2,1)S(1)} %node_update.1.refs_0_), channel_id=1, source_target_pairs={{0,4},{4,0},{8,12},{12,8},{16,20},{20,16},{24,28},{28,24},{1,5},{5... | collective-permute-start | bytes 393224 | tf_op jit(solution)/shard_map/ppermute | solution.py:32
  32.9 7.0 %collective-permute-start.11 = (bf16[512,128]{1,0:T(8,128)(2,1)S(1)}, bf16[512,128]{1,0:T(8,128)(2,1)S(1)}, u32[]{:S(2)}, u32[]{:S(2)}) collective-permute-start(bf16[512,128]{1,0:T(8,128)(2,1)S(1)} %node_update.1.refs_0_), channel_id=1, source_target_pairs={{0,8},{4,12},{8,24},{12,28},{16,0},{20,4},{24,16},{28,20},{1,9},{5... | collective-permute-start | bytes 393224 | tf_op jit(solution)/shard_map/ppermute | solution.py:35
  35.1 6.6 %collective-permute-start.15 = (bf16[512,128]{1,0:T(8,128)(2,1)S(1)}, bf16[512,128]{1,0:T(8,128)(2,1)S(1)}, u32[]{:S(2)}, u32[]{:S(2)}) collective-permute-start(bf16[512,128]{1,0:T(8,128)(2,1)S(1)} %collective-permute-done.13.refs_6_), channel_id=1, source_target_pairs={{0,4},{4,0},{8,12},{12,8},{16,20},{20,16},{24,28},{28,24},{1,5},{5... | collective-permute-start | bytes 393224 | tf_op jit(solution)/shard_map/ppermute | solution.py:32
  37.4 7.5 %collective-permute-start.14 = (bf16[512,128]{1,0:T(8,128)(2,1)S(1)}, bf16[512,128]{1,0:T(8,128)(2,1)S(1)}, u32[]{:S(2)}, u32[]{:S(2)}) collective-permute-start(bf16[512,128]{1,0:T(8,128)(2,1)S(1)} %collective-permute-done.13.refs_6_), channel_id=1, source_target_pairs={{0,16},{4,20},{8,0},{12,4},{16,24},{20,28},{24,8},{28,12},{1,17},{... | collective-permute-start | bytes 393224 | tf_op jit(solution)/shard_map/ppermute | solution.py:35
  39.9 5.0 %collective-permute-start.12 = (bf16[512,128]{1,0:T(8,128)(2,1)S(1)}, bf16[512,128]{1,0:T(8,128)(2,1)S(1)}, u32[]{:S(2)}, u32[]{:S(2)}) collective-permute-start(bf16[512,128]{1,0:T(8,128)(2,1)S(1)} %collective-permute-done.11.refs_2_), channel_id=1, source_target_pairs={{0,4},{4,0},{8,12},{12,8},{16,20},{20,16},{24,28},{28,24},{1,5},{5... | collective-permute-start | bytes 393224 | tf_op jit(solution)/shard_map/ppermute | solution.py:32
  41.6 5.0 %collective-permute-start.16 = (bf16[512,128]{1,0:T(8,128)(2,1)S(1)}, bf16[512,128]{1,0:T(8,128)(2,1)S(1)}, u32[]{:S(2)}, u32[]{:S(2)}) collective-permute-start(bf16[512,128]{1,0:T(8,128)(2,1)S(1)} %collective-permute-done.15.refs_7_), channel_id=1, source_target_pairs={{0,16},{4,20},{8,0},{12,4},{16,24},{20,28},{24,8},{28,12},{1,17},{... | collective-permute-start | bytes 393224 | tf_op jit(solution)/shard_map/ppermute | solution.py:35
  47.0 1.4 %collective-permute-start.17 = (bf16[512,128]{1,0:T(8,128)(2,1)S(1)}, bf16[512,128]{1,0:T(8,128)(2,1)S(1)}, u32[]{:S(2)}, u32[]{:S(2)}) collective-permute-start(bf16[512,128]{1,0:T(8,128)(2,1)S(1)} %get-tuple-element.31), channel_id=1, source_target_pairs={{0,1},{1,0},{2,3},{3,2},{4,5},{5,4},{6,7},{7,6},{8,9},{9,8},{10,11... | collective-permute-start | bytes 393224 | tf_op jit(solution)/shard_map/ppermute | solution.py:154
  48.4 5.6 %collective-permute-start.18 = (bf16[512,128]{1,0:T(8,128)(2,1)S(1)}, bf16[512,128]{1,0:T(8,128)(2,1)S(1)}, u32[]{:S(2)}, u32[]{:S(2)}) collective-permute-start(bf16[512,128]{1,0:T(8,128)(2,1)S(1)} %add_cores.3), channel_id=1, source_target_pairs={{0,2},{1,3},{2,0},{3,1},{4,6},{5,7},{6,4},{7,5},{8,10},{9,11},{10,... | collective-permute-start | bytes 393224 | tf_op jit(solution)/shard_map/ppermute | solution.py:160
  50.4 0.7 %copy-start.6 = (f32[128]{0:T(128)S(1)}, f32[128]{0:T(128)}, u32[]{:S(2)}) copy-start(f32[128]{0:T(128)} %param.14) | copy-start | bytes 1540
  50.9 3.2 %collective-permute-start.19 = (bf16[512,128]{1,0:T(8,128)(2,1)S(1)}, bf16[512,128]{1,0:T(8,128)(2,1)S(1)}, u32[]{:S(2)}, u32[]{:S(2)}) collective-permute-start(bf16[512,128]{1,0:T(8,128)(2,1)S(1)} %near_other.3), channel_id=1, source_target_pairs={{0,1},{1,0},{2,3},{3,2},{4,5},{5,4},{6,7},{7,6},{8,9},{9,8},{10,11... | collective-permute-start | bytes 393224 | tf_op jit(solution)/shard_map/ppermute | solution.py:163
where the time goes:
time: 55 us; the launch traced here: 54.8 us
  starting transfers between devices  30.4 us (55%)
  waiting for transfers between devices  15.6 us (28%)
  Pallas kernels  6.31 us (11%)
  local copies, waits for them, and re-layouts  1.75 us (3%)
  between operations  0.81 us (1%)
    ppermute x8, starting transfers between devices, step(): lax.ppermute(piece, 'blk', [(i, 2 * hop(i // 2) + i % 2) for i in range(n)])  18.7 us
    ppermute x6, starting transfers between devices, beside(): return lax.ppermute(piece, 'blk', [(i, i ^ 1) for i in range(n)])  8.22 us
    ppermute x8, waiting for transfers between devices, step(): lax.ppermute(piece, 'blk', [(i, 2 * hop(i // 2) + i % 2) for i in range(n)])  6.96 us
    ppermute x2, waiting for transfers between devices, tile_products(): far.append(lax.ppermute(part, 'rep', [(i, i ^ 2 * j) for i in range(reps)]))  4.85 us
    ppermute x2, starting transfers between devices, tile_products(): far.append(lax.ppermute(part, 'rep', [(i, i ^ 2 * j) for i in range(reps)]))  3.17 us
    pallas_call x6, Pallas kernels, sums(): pl.pallas_call(functools.partial(sums_kernel, owners), out_shape=jax.Shap...  2.41 us
    ppermute x6, waiting for transfers between devices, beside(): return lax.ppermute(piece, 'blk', [(i, i ^ 1) for i in range(n)])  1.91 us
    ppermute x2, waiting for transfers between devices, tile_products(): core = lax.ppermute(across, 'rep', other)  1.85 us
  transfers between devices with their start and end apart: 20, of which 10 were waited for; matrix products, arithmetic and copies ran while one was open for 0% of the time, Pallas kernels for 7%

commit v1 on v0

--- a/solution.py
+++ b/solution.py
@@ -217,7 +217,7 @@
 def node_pre(terms, rows, w_in, b_in):
     agg_b = add_terms(terms, rows).astype(jnp.bfloat16)
     pre = contract(agg_b, w_in[...], (1, 0)) + b_in[...]
-    return pre, 1.0 / (1.0 + jnp.exp(-pre))
+    return pre, 0.5 * jnp.tanh(0.5 * pre) + 0.5
 
 
 def node_kernel(n_terms, *refs):

time: 55 us -> 54.9 us (level)
  no operation moved by 1% of the time
where the time goes in v1:
time: 54.9 us; the launch traced here: 54.8 us
  starting transfers between devices  30.4 us (55%)
  waiting for transfers between devices  15.6 us (28%)
  Pallas kernels  6.24 us (11%)
  local copies, waits for them, and re-layouts  1.75 us (3%)
  between operations  0.8 us (1%)
    ppermute x8, starting transfers between devices, step(): lax.ppermute(piece, 'blk', [(i, 2 * hop(i // 2) + i % 2) for i in range(n)])  18.7 us
    ppermute x6, starting transfers between devices, beside(): return lax.ppermute(piece, 'blk', [(i, i ^ 1) for i in range(n)])  8.23 us
    ppermute x8, waiting for transfers between devices, step(): lax.ppermute(piece, 'blk', [(i, 2 * hop(i // 2) + i % 2) for i in range(n)])  6.95 us
    ppermute x2, waiting for transfers between devices, tile_products(): far.append(lax.ppermute(part, 'rep', [(i, i ^ 2 * j) for i in range(reps)]))  4.9 us
    ppermute x2, starting transfers between devices, tile_products(): far.append(lax.ppermute(part, 'rep', [(i, i ^ 2 * j) for i in range(reps)]))  3.17 us
    pallas_call x6, Pallas kernels, sums(): pl.pallas_call(functools.partial(sums_kernel, owners), out_shape=jax.Shap...  2.41 us
    ppermute x6, waiting for transfers between devices, beside(): return lax.ppermute(piece, 'blk', [(i, i ^ 1) for i in range(n)])  1.9 us
    ppermute x2, waiting for transfers between devices, tile_products(): core = lax.ppermute(across, 'rep', other)  1.85 us
  transfers between devices with their start and end apart: 20, of which 10 were waited for; matrix products, arithmetic and copies ran while one was open for 0% of the time, Pallas kernels for 7%

profile of v1, /device:TPU:0, one launch (start us, length us, event | category | flops | bytes accessed | tf_op | source)
XLA Modules:
  0.0 54.8 jit_solution(7218756758443661288)
XLA Ops:
  0.6 4.1 %collective-permute-start.3 = (bf16[512,128]{1,0:T(8,128)(2,1)}, bf16[512,128]{1,0:T(8,128)(2,1)S(1)}, u32[]{:S(2)}, u32[]{:S(2)}) collective-permute-start(bf16[512,128]{1,0:T(8,128)(2,1)} %refs_3_.2), channel_id=1, source_target_pairs={{0,16},{4,20},{8,0},{12,4},{16,24},{20,28},{24,8},{28,12},{1,17},{... | collective-permute-start | bytes 393224 | tf_op jit(solution)/shard_map/ppermute | solution.py:35
  4.7 1.5 %collective-permute-start = (bf16[512,128]{1,0:T(8,128)(2,1)}, bf16[512,128]{1,0:T(8,128)(2,1)S(1)}, u32[]{:S(2)}, u32[]{:S(2)}) collective-permute-start(bf16[512,128]{1,0:T(8,128)(2,1)} %refs_3_.2), channel_id=1, source_target_pairs={{0,4},{4,0},{8,12},{12,8},{16,20},{20,16},{24,28},{28,24},{1,5},{5... | collective-permute-start | bytes 393224 | tf_op jit(solution)/shard_map/ppermute | solution.py:32
  6.2 0.0 collective-permute-start.1
  6.2 2.7 %collective-permute-done.3.refs_6_ = bf16[512,128]{1,0:T(8,128)(2,1)S(1)} collective-permute-done((bf16[512,128]{1,0:T(8,128)(2,1)}, bf16[512,128]{1,0:T(8,128)(2,1)S(1)}, u32[]{:S(2)}, u32[]{:S(2)}) %collective-permute-start.3) | collective-permute-done | bytes 131104 | tf_op jit(solution)/shard_map/ppermute | solution.py:35
  8.9 1.5 %collective-permute-start.5 = (bf16[512,128]{1,0:T(8,128)(2,1)S(1)}, bf16[512,128]{1,0:T(8,128)(2,1)S(1)}, u32[]{:S(2)}, u32[]{:S(2)}) collective-permute-start(bf16[512,128]{1,0:T(8,128)(2,1)S(1)} %collective-permute-done.3.refs_6_), channel_id=1, source_target_pairs={{0,4},{4,0},{8,12},{12,8},{16,20},{20,16},{24,28},{28,24},{1,5},{5... | collective-permute-start | bytes 393224 | tf_op jit(solution)/shard_map/ppermute | solution.py:32
  10.4 0.0 collective-permute-done.refs_1_
  10.5 3.2 %collective-permute-start.4 = (bf16[512,128]{1,0:T(8,128)(2,1)S(1)}, bf16[512,128]{1,0:T(8,128)(2,1)S(1)}, u32[]{:S(2)}, u32[]{:S(2)}) collective-permute-start(bf16[512,128]{1,0:T(8,128)(2,1)S(1)} %collective-permute-done.3.refs_6_), channel_id=1, source_target_pairs={{0,16},{4,20},{8,0},{12,4},{16,24},{20,28},{24,8},{28,12},{1,17},{... | collective-permute-start | bytes 393224 | tf_op jit(solution)/shard_map/ppermute | solution.py:35
  13.7 0.0 collective-permute-done.1.refs_2_
  13.7 0.5 collective-permute-start.2
  14.2 0.0 collective-permute-done.5.refs_7_
  14.3 2.9 %collective-permute-start.6 = (bf16[512,128]{1,0:T(8,128)(2,1)S(1)}, bf16[512,128]{1,0:T(8,128)(2,1)S(1)}, u32[]{:S(2)}, u32[]{:S(2)}) collective-permute-start(bf16[512,128]{1,0:T(8,128)(2,1)S(1)} %collective-permute-done.5.refs_7_), channel_id=1, source_target_pairs={{0,16},{4,20},{8,0},{12,4},{16,24},{20,28},{24,8},{28,12},{1,17},{... | collective-permute-start | bytes 393224 | tf_op jit(solution)/shard_map/ppermute | solution.py:35
  17.2 0.7 %copy-done.7 = s32[16,1,4]{0,2,1:T(4,128)S(1)} copy-done((s32[16,1,4]{0,2,1:T(4,128)S(1)}, s32[16,1,4]{0,2,1:T(4,128)}, u32[]{:S(2)}) %copy-start.7) | copy-done | bytes 280
  17.9 0.1 by_row.1.columns
  17.9 0.8 %copy-done.1 = bf16[512,128]{1,0:T(8,128)(2,1)S(1)} copy-done((bf16[512,128]{1,0:T(8,128)(2,1)S(1)}, bf16[512,128]{1,0:T(8,128)(2,1)}, u32[]{:S(2)}) %copy-start.1) | copy-done | bytes 131096
  18.8 0.1 copy-done.4
  18.8 0.3 early.1.refs_3_
  19.1 0.0 collective-permute-done.2.refs_3_
  19.1 0.0 collective-permute-done.4.refs_4_
  19.1 0.6 %collective-permute-done.6.refs_5_ = bf16[512,128]{1,0:T(8,128)(2,1)S(1)} collective-permute-done((bf16[512,128]{1,0:T(8,128)(2,1)S(1)}, bf16[512,128]{1,0:T(8,128)(2,1)S(1)}, u32[]{:S(2)}, u32[]{:S(2)}) %collective-permute-start.6) | collective-permute-done | bytes 131104 | tf_op jit(solution)/shard_map/ppermute | solution.py:35
  19.7 0.0 copy-done
  19.7 0.0 copy-done.2
  19.7 0.4 other_sums.2
  20.1 0.1 collective-permute-start.7
  20.2 0.4 own_far.2.own
  20.6 0.9 %collective-permute-done.7.core = bf16[512,128]{1,0:T(8,128)(2,1)S(1)} collective-permute-done((bf16[512,128]{1,0:T(8,128)(2,1)S(1)}, bf16[512,128]{1,0:T(8,128)(2,1)S(1)}, u32[]{:S(2)}, u32[]{:S(2)}) %collective-permute-start.7) | collective-permute-done | bytes 131104 | tf_op jit(solution)/shard_map/ppermute | solution.py:154
  21.6 1.6 %collective-permute-start.8 = (bf16[512,128]{1,0:T(8,128)(2,1)S(1)}, bf16[512,128]{1,0:T(8,128)(2,1)S(1)}, u32[]{:S(2)}, u32[]{:S(2)}) collective-permute-start(bf16[512,128]{1,0:T(8,128)(2,1)S(1)} %add_cores.2), channel_id=1, source_target_pairs={{0,2},{1,3},{2,0},{3,1},{4,6},{5,7},{6,4},{7,5},{8,10},{9,11},{10,... | collective-permute-start | bytes 393224 | tf_op jit(solution)/shard_map/ppermute | solution.py:160
  23.2 0.4 own_near.2.refs_0_
  23.6 0.0 copy-start.3
  23.6 0.0 copy-start.5
  23.6 0.4 near_other.2
  24.0 0.1 collective-permute-start.9
  24.1 3.1 %collective-permute-done.8.refs_1_ = bf16[512,128]{1,0:T(8,128)(2,1)S(1)} collective-permute-done((bf16[512,128]{1,0:T(8,128)(2,1)S(1)}, bf16[512,128]{1,0:T(8,128)(2,1)S(1)}, u32[]{:S(2)}, u32[]{:S(2)}) %collective-permute-start.8) | collective-permute-done | bytes 131104 | tf_op jit(solution)/shard_map/ppermute | solution.py:160
  27.2 0.0 collective-permute-done.9.refs_2_
  27.2 0.0 copy-done.3
  27.2 0.0 copy-done.5
  27.2 0.7 %node_update.1.refs_0_ = bf16[512,128]{1,0:T(8,128)(2,1)S(1)} custom-call(f32[512,128]{1,0:T(8,128)S(1)} %own_near.2.refs_0_, bf16[512,128]{1,0:T(8,128)(2,1)S(1)} %collective-permute-done.8.refs_1_, bf16[512,128]{1,0:T(8,128)(2,1)S(1)} %collective-permute-done.9.refs_2_, f32[512,512]{1,0:T(8,128)S(1)} %early.1.refs_3_, bf16[128,512]{1,0:T(8,128)(2,1)S(1)} %copy-done.3, ...), custom_call_target="tpu_custom_call" | custom-call | flops 134217728 | bytes 2097152 | tf_op jit(solution)/shard_map/node_update/pallas_call | solution.py:234
  27.9 3.4 %collective-permute-start.13 = (bf16[512,128]{1,0:T(8,128)(2,1)S(1)}, bf16[512,128]{1,0:T(8,128)(2,1)S(1)}, u32[]{:S(2)}, u32[]{:S(2)}) collective-permute-start(bf16[512,128]{1,0:T(8,128)(2,1)S(1)} %node_update.1.refs_0_), channel_id=1, source_target_pairs={{0,16},{4,20},{8,0},{12,4},{16,24},{20,28},{24,8},{28,12},{1,17},{... | collective-permute-start | bytes 393224 | tf_op jit(solution)/shard_map/ppermute | solution.py:35
  31.3 1.5 %collective-permute-start.10 = (bf16[512,128]{1,0:T(8,128)(2,1)S(1)}, bf16[512,128]{1,0:T(8,128)(2,1)S(1)}, u32[]{:S(2)}, u32[]{:S(2)}) collective-permute-start(bf16[512,128]{1,0:T(8,128)(2,1)S(1)} %node_update.1.refs_0_), channel_id=1, source_target_pairs={{0,4},{4,0},{8,12},{12,8},{16,20},{20,16},{24,28},{28,24},{1,5},{5... | collective-permute-start | bytes 393224 | tf_op jit(solution)/shard_map/ppermute | solution.py:32
  32.8 0.2 collective-permute-start.11
  33.1 2.0 %collective-permute-done.13.refs_6_ = bf16[512,128]{1,0:T(8,128)(2,1)S(1)} collective-permute-done((bf16[512,128]{1,0:T(8,128)(2,1)S(1)}, bf16[512,128]{1,0:T(8,128)(2,1)S(1)}, u32[]{:S(2)}, u32[]{:S(2)}) %collective-permute-start.13) | collective-permute-done | bytes 131104 | tf_op jit(solution)/shard_map/ppermute | solution.py:35
  35.0 1.5 %collective-permute-start.15 = (bf16[512,128]{1,0:T(8,128)(2,1)S(1)}, bf16[512,128]{1,0:T(8,128)(2,1)S(1)}, u32[]{:S(2)}, u32[]{:S(2)}) collective-permute-start(bf16[512,128]{1,0:T(8,128)(2,1)S(1)} %collective-permute-done.13.refs_6_), channel_id=1, source_target_pairs={{0,4},{4,0},{8,12},{12,8},{16,20},{20,16},{24,28},{28,24},{1,5},{5... | collective-permute-start | bytes 393224 | tf_op jit(solution)/shard_map/ppermute | solution.py:32
  36.5 0.9 %collective-permute-done.10.refs_1_ = bf16[512,128]{1,0:T(8,128)(2,1)S(1)} collective-permute-done((bf16[512,128]{1,0:T(8,128)(2,1)S(1)}, bf16[512,128]{1,0:T(8,128)(2,1)S(1)}, u32[]{:S(2)}, u32[]{:S(2)}) %collective-permute-start.10) | collective-permute-done | bytes 131104 | tf_op jit(solution)/shard_map/ppermute | solution.py:32
  37.3 2.5 %collective-permute-start.14 = (bf16[512,128]{1,0:T(8,128)(2,1)S(1)}, bf16[512,128]{1,0:T(8,128)(2,1)S(1)}, u32[]{:S(2)}, u32[]{:S(2)}) collective-permute-start(bf16[512,128]{1,0:T(8,128)(2,1)S(1)} %collective-permute-done.13.refs_6_), channel_id=1, source_target_pairs={{0,16},{4,20},{8,0},{12,4},{16,24},{20,28},{24,8},{28,12},{1,17},{... | collective-permute-start | bytes 393224 | tf_op jit(solution)/shard_map/ppermute | solution.py:35
  39.9 0.0 collective-permute-done.11.refs_2_
  39.9 1.7 %collective-permute-start.12 = (bf16[512,128]{1,0:T(8,128)(2,1)S(1)}, bf16[512,128]{1,0:T(8,128)(2,1)S(1)}, u32[]{:S(2)}, u32[]{:S(2)}) collective-permute-start(bf16[512,128]{1,0:T(8,128)(2,1)S(1)} %collective-permute-done.11.refs_2_), channel_id=1, source_target_pairs={{0,4},{4,0},{8,12},{12,8},{16,20},{20,16},{24,28},{28,24},{1,5},{5... | collective-permute-start | bytes 393224 | tf_op jit(solution)/shard_map/ppermute | solution.py:32
  41.6 0.0 collective-permute-done.15.refs_7_
  41.6 2.3 %collective-permute-start.16 = (bf16[512,128]{1,0:T(8,128)(2,1)S(1)}, bf16[512,128]{1,0:T(8,128)(2,1)S(1)}, u32[]{:S(2)}, u32[]{:S(2)}) collective-permute-start(bf16[512,128]{1,0:T(8,128)(2,1)S(1)} %collective-permute-done.15.refs_7_), channel_id=1, source_target_pairs={{0,16},{4,20},{8,0},{12,4},{16,24},{20,28},{24,8},{28,12},{1,17},{... | collective-permute-start | bytes 393224 | tf_op jit(solution)/shard_map/ppermute | solution.py:35
  43.8 1.0 %collective-permute-done.12.refs_3_ = bf16[512,128]{1,0:T(8,128)(2,1)S(1)} collective-permute-done((bf16[512,128]{1,0:T(8,128)(2,1)S(1)}, bf16[512,128]{1,0:T(8,128)(2,1)S(1)}, u32[]{:S(2)}, u32[]{:S(2)}) %collective-permute-start.12) | collective-permute-done | bytes 131104 | tf_op jit(solution)/shard_map/ppermute | solution.py:32
  44.8 0.0 collective-permute-done.14.refs_4_
  44.8 1.7 %collective-permute-done.16.refs_5_ = bf16[512,128]{1,0:T(8,128)(2,1)S(1)} collective-permute-done((bf16[512,128]{1,0:T(8,128)(2,1)S(1)}, bf16[512,128]{1,0:T(8,128)(2,1)S(1)}, u32[]{:S(2)}, u32[]{:S(2)}) %collective-permute-start.16) | collective-permute-done | bytes 131104 | tf_op jit(solution)/shard_map/ppermute | solution.py:35
  46.6 0.4 other_sums.3
  47.0 0.1 collective-permute-start.17
  47.1 0.4 own_far.3.own
  47.5 0.9 %collective-permute-done.17.core = bf16[512,128]{1,0:T(8,128)(2,1)S(1)} collective-permute-done((bf16[512,128]{1,0:T(8,128)(2,1)S(1)}, bf16[512,128]{1,0:T(8,128)(2,1)S(1)}, u32[]{:S(2)}, u32[]{:S(2)}) %collective-permute-start.17) | collective-permute-done | bytes 131104 | tf_op jit(solution)/shard_map/ppermute | solution.py:154
  48.4 1.6 %collective-permute-start.18 = (bf16[512,128]{1,0:T(8,128)(2,1)S(1)}, bf16[512,128]{1,0:T(8,128)(2,1)S(1)}, u32[]{:S(2)}, u32[]{:S(2)}) collective-permute-start(bf16[512,128]{1,0:T(8,128)(2,1)S(1)} %add_cores.3), channel_id=1, source_target_pairs={{0,2},{1,3},{2,0},{3,1},{4,6},{5,7},{6,4},{7,5},{8,10},{9,11},{10,... | collective-permute-start | bytes 393224 | tf_op jit(solution)/shard_map/ppermute | solution.py:160
  50.0 0.4 own_near.3.refs_0_
  50.4 0.0 copy-start.6
  50.4 0.4 near_other.3
  50.8 0.1 collective-permute-start.19
  50.9 0.2 copy-done.6
  51.1 1.2 %project.1 = bf16[512,128]{1,0:T(8,128)(2,1)} custom-call(f32[512,128]{1,0:T(8,128)S(1)} %own_near.2.refs_0_, bf16[512,128]{1,0:T(8,128)(2,1)S(1)} %collective-permute-done.8.refs_1_, bf16[512,128]{1,0:T(8,128)(2,1)S(1)} %collective-permute-done.9.refs_2_, bf16[512,128]{1,0:T(8,128)(2,1)S(1)} %copy-done.2, bf16[128,512]{1,0:T(8,128)(2,1)S(1)} %copy-done.3, ...), custom_call_target="tpu_custom_call" | custom-call | flops 134217728 | bytes 524288 | tf_op jit(solution)/shard_map/project/pallas_call | solution.py:258
  52.2 1.8 %collective-permute-done.18.refs_1_ = bf16[512,128]{1,0:T(8,128)(2,1)S(1)} collective-permute-done((bf16[512,128]{1,0:T(8,128)(2,1)S(1)}, bf16[512,128]{1,0:T(8,128)(2,1)S(1)}, u32[]{:S(2)}, u32[]{:S(2)}) %collective-permute-start.18) | collective-permute-done | bytes 131104 | tf_op jit(solution)/shard_map/ppermute | solution.py:160
  54.0 0.0 collective-permute-done.19.refs_2_
  54.0 0.7 %close_grad.1 = bf16[512,128]{1,0:T(8,128)(2,1)} custom-call(f32[512,128]{1,0:T(8,128)S(1)} %own_near.3.refs_0_, bf16[512,128]{1,0:T(8,128)(2,1)S(1)} %collective-permute-done.18.refs_1_, bf16[512,128]{1,0:T(8,128)(2,1)S(1)} %collective-permute-done.19.refs_2_, bf16[512,128]{1,0:T(8,128)(2,1)S(1)} %copy-done.1), custom_call_target="tpu_custom_call" | custom-call | tf_op jit(solution)/shard_map/close_grad/pallas_call | solution.py:278
  (7 shorter events, 0.1 us)
Async XLA Ops:
  0.6 8.3 %collective-permute-start.3 = (bf16[512,128]{1,0:T(8,128)(2,1)}, bf16[512,128]{1,0:T(8,128)(2,1)S(1)}, u32[]{:S(2)}, u32[]{:S(2)}) collective-permute-start(bf16[512,128]{1,0:T(8,128)(2,1)} %refs_3_.2), channel_id=1, source_target_pairs={{0,16},{4,20},{8,0},{12,4},{16,24},{20,28},{24,8},{28,12},{1,17},{... | collective-permute-start | bytes 393224 | tf_op jit(solution)/shard_map/ppermute | solution.py:35
  4.7 5.7 %collective-permute-start = (bf16[512,128]{1,0:T(8,128)(2,1)}, bf16[512,128]{1,0:T(8,128)(2,1)S(1)}, u32[]{:S(2)}, u32[]{:S(2)}) collective-permute-start(bf16[512,128]{1,0:T(8,128)(2,1)} %refs_3_.2), channel_id=1, source_target_pairs={{0,4},{4,0},{8,12},{12,8},{16,20},{20,16},{24,28},{28,24},{1,5},{5... | collective-permute-start | bytes 393224 | tf_op jit(solution)/shard_map/ppermute | solution.py:32
  6.2 7.5 %collective-permute-start.1 = (bf16[512,128]{1,0:T(8,128)(2,1)}, bf16[512,128]{1,0:T(8,128)(2,1)S(1)}, u32[]{:S(2)}, u32[]{:S(2)}) collective-permute-start(bf16[512,128]{1,0:T(8,128)(2,1)} %refs_3_.2), channel_id=1, source_target_pairs={{0,8},{4,12},{8,24},{12,28},{16,0},{20,4},{24,16},{28,20},{1,9},{5... | collective-permute-start | bytes 393224 | tf_op jit(solution)/shard_map/ppermute | solution.py:35
  8.9 5.3 %collective-permute-start.5 = (bf16[512,128]{1,0:T(8,128)(2,1)S(1)}, bf16[512,128]{1,0:T(8,128)(2,1)S(1)}, u32[]{:S(2)}, u32[]{:S(2)}) collective-permute-start(bf16[512,128]{1,0:T(8,128)(2,1)S(1)} %collective-permute-done.3.refs_6_), channel_id=1, source_target_pairs={{0,4},{4,0},{8,12},{12,8},{16,20},{20,16},{24,28},{28,24},{1,5},{5... | collective-permute-start | bytes 393224 | tf_op jit(solution)/shard_map/ppermute | solution.py:32
  10.5 8.7 %collective-permute-start.4 = (bf16[512,128]{1,0:T(8,128)(2,1)S(1)}, bf16[512,128]{1,0:T(8,128)(2,1)S(1)}, u32[]{:S(2)}, u32[]{:S(2)}) collective-permute-start(bf16[512,128]{1,0:T(8,128)(2,1)S(1)} %collective-permute-done.3.refs_6_), channel_id=1, source_target_pairs={{0,16},{4,20},{8,0},{12,4},{16,24},{20,28},{24,8},{28,12},{1,17},{... | collective-permute-start | bytes 393224 | tf_op jit(solution)/shard_map/ppermute | solution.py:35
  13.7 5.4 %collective-permute-start.2 = (bf16[512,128]{1,0:T(8,128)(2,1)S(1)}, bf16[512,128]{1,0:T(8,128)(2,1)S(1)}, u32[]{:S(2)}, u32[]{:S(2)}) collective-permute-start(bf16[512,128]{1,0:T(8,128)(2,1)S(1)} %collective-permute-done.1.refs_2_), channel_id=1, source_target_pairs={{0,4},{4,0},{8,12},{12,8},{16,20},{20,16},{24,28},{28,24},{1,5},{5... | collective-permute-start | bytes 393224 | tf_op jit(solution)/shard_map/ppermute | solution.py:32
  14.3 5.5 %collective-permute-start.6 = (bf16[512,128]{1,0:T(8,128)(2,1)S(1)}, bf16[512,128]{1,0:T(8,128)(2,1)S(1)}, u32[]{:S(2)}, u32[]{:S(2)}) collective-permute-start(bf16[512,128]{1,0:T(8,128)(2,1)S(1)} %collective-permute-done.5.refs_7_), channel_id=1, source_target_pairs={{0,16},{4,20},{8,0},{12,4},{16,24},{20,28},{24,8},{28,12},{1,17},{... | collective-permute-start | bytes 393224 | tf_op jit(solution)/shard_map/ppermute | solution.py:35
  17.2 0.7 %copy-start.7 = (s32[16,1,4]{0,2,1:T(4,128)S(1)}, s32[16,1,4]{0,2,1:T(4,128)}, u32[]{:S(2)}) copy-start(s32[16,1,4]{0,2,1:T(4,128)} %param.10) | copy-start | bytes 772
  17.9 0.9 %copy-start.1 = (bf16[512,128]{1,0:T(8,128)(2,1)S(1)}, bf16[512,128]{1,0:T(8,128)(2,1)}, u32[]{:S(2)}) copy-start(bf16[512,128]{1,0:T(8,128)(2,1)} %refs_3_.3) | copy-start | bytes 393220
  17.9 1.0 %copy-start.4 = (bf16[512,128]{1,0:T(8,128)(2,1)S(1)}, bf16[512,128]{1,0:T(8,128)(2,1)}, u32[]{:S(2)}) copy-start(bf16[512,128]{1,0:T(8,128)(2,1)} %refs_6_.1) | copy-start | bytes 393220
  17.9 1.8 %copy-start = (bf16[16,1,4,128,128]{4,3,2,1,0:T(8,128)(2,1)S(1)}, bf16[16,1,4,128,128]{4,3,2,1,0:T(8,128)(2,1)}, u32[]{:S(2)}) copy-start(bf16[16,1,4,128,128]{4,3,2,1,0:T(8,128)(2,1)} %tiles.15) | copy-start | bytes 6291460
  17.9 1.8 %copy-start.2 = (bf16[512,128]{1,0:T(8,128)(2,1)S(1)}, bf16[512,128]{1,0:T(8,128)(2,1)}, u32[]{:S(2)}) copy-start(bf16[512,128]{1,0:T(8,128)(2,1)} %refs_3_.2) | copy-start | bytes 393220
  20.1 1.4 %collective-permute-start.7 = (bf16[512,128]{1,0:T(8,128)(2,1)S(1)}, bf16[512,128]{1,0:T(8,128)(2,1)S(1)}, u32[]{:S(2)}, u32[]{:S(2)}) collective-permute-start(bf16[512,128]{1,0:T(8,128)(2,1)S(1)} %get-tuple-element.23), channel_id=1, source_target_pairs={{0,1},{1,0},{2,3},{3,2},{4,5},{5,4},{6,7},{7,6},{8,9},{9,8},{10,11... | collective-permute-start | bytes 393224 | tf_op jit(solution)/shard_map/ppermute | solution.py:154
  21.6 5.6 %collective-permute-start.8 = (bf16[512,128]{1,0:T(8,128)(2,1)S(1)}, bf16[512,128]{1,0:T(8,128)(2,1)S(1)}, u32[]{:S(2)}, u32[]{:S(2)}) collective-permute-start(bf16[512,128]{1,0:T(8,128)(2,1)S(1)} %add_cores.2), channel_id=1, source_target_pairs={{0,2},{1,3},{2,0},{3,1},{4,6},{5,7},{6,4},{7,5},{8,10},{9,11},{10,... | collective-permute-start | bytes 393224 | tf_op jit(solution)/shard_map/ppermute | solution.py:160
  23.6 3.6 %copy-start.3 = (bf16[128,512]{1,0:T(8,128)(2,1)S(1)}, bf16[128,512]{1,0:T(8,128)(2,1)}, u32[]{:S(2)}) copy-start(bf16[128,512]{1,0:T(8,128)(2,1)} %refs_4_.3) | copy-start | bytes 393220
  23.6 3.6 %copy-start.5 = (f32[512]{0:T(512)S(1)}, f32[512]{0:T(512)}, u32[]{:S(2)}) copy-start(f32[512]{0:T(512)} %param.12) | copy-start | bytes 6148
  24.0 3.2 %collective-permute-start.9 = (bf16[512,128]{1,0:T(8,128)(2,1)S(1)}, bf16[512,128]{1,0:T(8,128)(2,1)S(1)}, u32[]{:S(2)}, u32[]{:S(2)}) collective-permute-start(bf16[512,128]{1,0:T(8,128)(2,1)S(1)} %near_other.2), channel_id=1, source_target_pairs={{0,1},{1,0},{2,3},{3,2},{4,5},{5,4},{6,7},{7,6},{8,9},{9,8},{10,11... | collective-permute-start | bytes 393224 | tf_op jit(solution)/shard_map/ppermute | solution.py:163
  27.9 7.1 %collective-permute-start.13 = (bf16[512,128]{1,0:T(8,128)(2,1)S(1)}, bf16[512,128]{1,0:T(8,128)(2,1)S(1)}, u32[]{:S(2)}, u32[]{:S(2)}) collective-permute-start(bf16[512,128]{1,0:T(8,128)(2,1)S(1)} %node_update.1.refs_0_), channel_id=1, source_target_pairs={{0,16},{4,20},{8,0},{12,4},{16,24},{20,28},{24,8},{28,12},{1,17},{... | collective-permute-start | bytes 393224 | tf_op jit(solution)/shard_map/ppermute | solution.py:35
  31.3 6.1 %collective-permute-start.10 = (bf16[512,128]{1,0:T(8,128)(2,1)S(1)}, bf16[512,128]{1,0:T(8,128)(2,1)S(1)}, u32[]{:S(2)}, u32[]{:S(2)}) collective-permute-start(bf16[512,128]{1,0:T(8,128)(2,1)S(1)} %node_update.1.refs_0_), channel_id=1, source_target_pairs={{0,4},{4,0},{8,12},{12,8},{16,20},{20,16},{24,28},{28,24},{1,5},{5... | collective-permute-start | bytes 393224 | tf_op jit(solution)/shard_map/ppermute | solution.py:32
  32.8 7.0 %collective-permute-start.11 = (bf16[512,128]{1,0:T(8,128)(2,1)S(1)}, bf16[512,128]{1,0:T(8,128)(2,1)S(1)}, u32[]{:S(2)}, u32[]{:S(2)}) collective-permute-start(bf16[512,128]{1,0:T(8,128)(2,1)S(1)} %node_update.1.refs_0_), channel_id=1, source_target_pairs={{0,8},{4,12},{8,24},{12,28},{16,0},{20,4},{24,16},{28,20},{1,9},{5... | collective-permute-start | bytes 393224 | tf_op jit(solution)/shard_map/ppermute | solution.py:35
  35.0 6.6 %collective-permute-start.15 = (bf16[512,128]{1,0:T(8,128)(2,1)S(1)}, bf16[512,128]{1,0:T(8,128)(2,1)S(1)}, u32[]{:S(2)}, u32[]{:S(2)}) collective-permute-start(bf16[512,128]{1,0:T(8,128)(2,1)S(1)} %collective-permute-done.13.refs_6_), channel_id=1, source_target_pairs={{0,4},{4,0},{8,12},{12,8},{16,20},{20,16},{24,28},{28,24},{1,5},{5... | collective-permute-start | bytes 393224 | tf_op jit(solution)/shard_map/ppermute | solution.py:32
  37.3 7.5 %collective-permute-start.14 = (bf16[512,128]{1,0:T(8,128)(2,1)S(1)}, bf16[512,128]{1,0:T(8,128)(2,1)S(1)}, u32[]{:S(2)}, u32[]{:S(2)}) collective-permute-start(bf16[512,128]{1,0:T(8,128)(2,1)S(1)} %collective-permute-done.13.refs_6_), channel_id=1, source_target_pairs={{0,16},{4,20},{8,0},{12,4},{16,24},{20,28},{24,8},{28,12},{1,17},{... | collective-permute-start | bytes 393224 | tf_op jit(solution)/shard_map/ppermute | solution.py:35
  39.9 5.0 %collective-permute-start.12 = (bf16[512,128]{1,0:T(8,128)(2,1)S(1)}, bf16[512,128]{1,0:T(8,128)(2,1)S(1)}, u32[]{:S(2)}, u32[]{:S(2)}) collective-permute-start(bf16[512,128]{1,0:T(8,128)(2,1)S(1)} %collective-permute-done.11.refs_2_), channel_id=1, source_target_pairs={{0,4},{4,0},{8,12},{12,8},{16,20},{20,16},{24,28},{28,24},{1,5},{5... | collective-permute-start | bytes 393224 | tf_op jit(solution)/shard_map/ppermute | solution.py:32
  41.6 5.0 %collective-permute-start.16 = (bf16[512,128]{1,0:T(8,128)(2,1)S(1)}, bf16[512,128]{1,0:T(8,128)(2,1)S(1)}, u32[]{:S(2)}, u32[]{:S(2)}) collective-permute-start(bf16[512,128]{1,0:T(8,128)(2,1)S(1)} %collective-permute-done.15.refs_7_), channel_id=1, source_target_pairs={{0,16},{4,20},{8,0},{12,4},{16,24},{20,28},{24,8},{28,12},{1,17},{... | collective-permute-start | bytes 393224 | tf_op jit(solution)/shard_map/ppermute | solution.py:35
  47.0 1.4 %collective-permute-start.17 = (bf16[512,128]{1,0:T(8,128)(2,1)S(1)}, bf16[512,128]{1,0:T(8,128)(2,1)S(1)}, u32[]{:S(2)}, u32[]{:S(2)}) collective-permute-start(bf16[512,128]{1,0:T(8,128)(2,1)S(1)} %get-tuple-element.31), channel_id=1, source_target_pairs={{0,1},{1,0},{2,3},{3,2},{4,5},{5,4},{6,7},{7,6},{8,9},{9,8},{10,11... | collective-permute-start | bytes 393224 | tf_op jit(solution)/shard_map/ppermute | solution.py:154
  48.4 5.6 %collective-permute-start.18 = (bf16[512,128]{1,0:T(8,128)(2,1)S(1)}, bf16[512,128]{1,0:T(8,128)(2,1)S(1)}, u32[]{:S(2)}, u32[]{:S(2)}) collective-permute-start(bf16[512,128]{1,0:T(8,128)(2,1)S(1)} %add_cores.3), channel_id=1, source_target_pairs={{0,2},{1,3},{2,0},{3,1},{4,6},{5,7},{6,4},{7,5},{8,10},{9,11},{10,... | collective-permute-start | bytes 393224 | tf_op jit(solution)/shard_map/ppermute | solution.py:160
  50.4 0.7 %copy-start.6 = (f32[128]{0:T(128)S(1)}, f32[128]{0:T(128)}, u32[]{:S(2)}) copy-start(f32[128]{0:T(128)} %param.14) | copy-start | bytes 1540
  50.8 3.2 %collective-permute-start.19 = (bf16[512,128]{1,0:T(8,128)(2,1)S(1)}, bf16[512,128]{1,0:T(8,128)(2,1)S(1)}, u32[]{:S(2)}, u32[]{:S(2)}) collective-permute-start(bf16[512,128]{1,0:T(8,128)(2,1)S(1)} %near_other.3), channel_id=1, source_target_pairs={{0,1},{1,0},{2,3},{3,2},{4,5},{5,4},{6,7},{7,6},{8,9},{9,8},{10,11... | collective-permute-start | bytes 393224 | tf_op jit(solution)/shard_map/ppermute | solution.py:163
